TPU v7x, 256 devices: a whole 4x4x8 slice. The times are simulated.
256 devices in a mesh: tm: 16 (over z, core), height: 8 (over x, y_hi), batch: 2 (over y_lo).
Axes of the slice: x: 4, y: 4 (y_hi: 2, y_lo: 2; y = y_hi * 2 + y_lo), z: 8, core: 2. Of those that a mesh axis runs over, the one named last changes fastest.
Arguments:
- features: bfloat16 [2, 64, 64, 64, 256], P('batch', None, 'tm', 'height'), may hold values from -6 to 6
- cotangent: bfloat16 [2, 64, 64, 64, 256], P('batch', None, 'tm', 'height'), may hold values from -6 to 6
- w_spatial: bfloat16 [3, 3, 64, 64], replicated, may hold values from -0.25 to 0.25
- w_first: bfloat16 [3, 64, 64], replicated, may hold values from -0.4375 to 0.4375
- w_second: bfloat16 [3, 64, 64], replicated, may hold values from -0.4375 to 0.4375
Outputs:
- input_grad: bfloat16 [2, 64, 64, 64, 256], P('batch', None, 'tm', 'height')
- grad_spatial: float32 [3, 3, 64, 64], replicated
- grad_first: float32 [3, 64, 64], replicated
- grad_second: float32 [3, 64, 64], replicated
All inputs are finite; a program needn't handle non-finite values.
Results may differ from a plain program's by a relative error of at most 0.0058.
Values may be sent and summed in bfloat16 or wider, within the bound.
A program may use at most 64 MiB of HBM per device.

v0:
```python
import math

import jax
import jax.numpy as jnp
from jax import lax
from jax.sharding import PartitionSpec as P


def extended(block, sides, width, periodic):
    for axis, dim in sides:
        count = lax.axis_size(axis)
        forward = [(i, i + 1) for i in range(count - 1)]
        if periodic:
            forward.append((count - 1, 0))
        backward = [(target, source) for source, target in forward]
        low = lax.ppermute(
            lax.slice_in_dim(block, block.shape[dim] - width, None, axis=dim), axis, forward
        )
        high = lax.ppermute(lax.slice_in_dim(block, 0, width, axis=dim), axis, backward)
        block = jnp.concatenate([low, block, high], axis=dim)
    return block


def activate(value):
    return 0.2 * value + 0.8 * value * jax.nn.sigmoid(value)


def derivative(value):
    sig = jax.nn.sigmoid(value)
    return 0.2 + 0.8 * sig * (1.0 + value * (1.0 - sig))


def shift_cols(value, step):
    if step == 0:
        return value
    zeros = jnp.zeros(value.shape[:-1] + (abs(step),), value.dtype)
    if step > 0:
        return jnp.concatenate([value[..., step:], zeros], axis=-1)
    return jnp.concatenate([zeros, value[..., :step]], axis=-1)


def mix(weight, value):
    return jnp.einsum("oc,bcfhw->bofhw", weight, value, preferred_element_type=jnp.float32)


def back(weight, value):
    return jnp.einsum("oc,bofhw->bcfhw", weight, value, preferred_element_type=jnp.float32)


def outer(grads, value):
    return jnp.einsum("bofhw,bcfhw->oc", grads, value, preferred_element_type=jnp.float32)


def edge_rows(value):
    return extended(value, (("height", 3),), 1, False)


def cycle_frames(value, width):
    return extended(value, (("tm", 2),), width, True)


def per_device(features, cotangent, w_spatial, w_first, w_second):
    nframes = features.shape[2]
    nrows = features.shape[3]
    rows_wide = edge_rows(features)
    moved_cols = [shift_cols(rows_wide, j - 1) for j in range(3)]
    first_pre = jnp.zeros(features.shape, jnp.float32)
    for j in range(3):
        for i in range(3):
            first_pre = first_pre + mix(w_spatial[i, j], moved_cols[j][:, :, :, i : i + nrows])
    first = activate(first_pre).astype(jnp.bfloat16)
    first_wide = cycle_frames(first, 1)
    second_pre = jnp.zeros(first.shape, jnp.float32)
    for k in range(3):
        second_pre = second_pre + mix(w_first[k], first_wide[:, :, k : k + nframes])
    second = activate(second_pre).astype(jnp.bfloat16)
    second_wide = cycle_frames(second, 2)
    cot_wide = cycle_frames(cotangent, 2)
    summed_back = jnp.zeros(first.shape, jnp.float32)
    for k in range(3):
        summed_back = summed_back + back(
            w_second[k], cot_wide[:, :, 4 - 2 * k : 4 - 2 * k + nframes]
        )
    second_back = (summed_back * derivative(second_pre)).astype(jnp.bfloat16)
    second_back_wide = cycle_frames(second_back, 1)
    total = jnp.zeros(first.shape, jnp.float32)
    for k in range(3):
        total = total + back(w_first[k], second_back_wide[:, :, 2 - k : 2 - k + nframes])
    first_back = (total * derivative(first_pre)).astype(jnp.bfloat16)
    grad_second = jnp.stack(
        [outer(cotangent, second_wide[:, :, 2 * k : 2 * k + nframes]) for k in range(3)]
    )
    grad_first = jnp.stack(
        [outer(second_back, first_wide[:, :, k : k + nframes]) for k in range(3)]
    )
    grad_spatial = jnp.stack(
        [
            jnp.stack([outer(first_back, moved_cols[j][:, :, :, i : i + nrows]) for j in range(3)])
            for i in range(3)
        ]
    )
    back_wide = edge_rows(first_back)
    total = jnp.zeros(features.shape, jnp.float32)
    for i in range(3):
        for j in range(3):
            moved = shift_cols(back_wide[:, :, :, 2 - i : 2 - i + nrows], 1 - j)
            total = total + back(w_spatial[i, j], moved)
    input_grad = total.astype(jnp.bfloat16)
    summed = lax.psum((grad_spatial, grad_first, grad_second), ("tm", "height", "batch"))
    count = (
        features.shape[0]
        * lax.axis_size("batch")
        * nframes
        * lax.axis_size("tm")
        * nrows
        * lax.axis_size("height")
        * features.shape[4]
    )
    scale = 1.0 / math.sqrt(count)
    return (input_grad, summed[0] * scale, summed[1] * scale, summed[2] * scale)


def solution(mesh):
    in_specs = (
        P("batch", None, "tm", "height", None),
        P("batch", None, "tm", "height", None),
        P(),
        P(),
        P(),
    )
    out_specs = (P("batch", None, "tm", "height", None), P(), P(), P())
    return jax.shard_map(
        per_device, mesh=mesh, in_specs=in_specs, out_specs=out_specs, check_vma=False
    )
```

profile of v0, /device:TPU:1, one launch (start us, length us, event | category | flops | bytes accessed | tf_op | source)
XLA Modules:
  0.0 583.9 jit_solution(3583388901304782319)
XLA Ops:
  7.2 1.9 copy.17
  9.1 5.7 collective-permute-start.2
  27.5 3.7 collective-permute-start.4
  31.6 2.9 collective-permute-done.4
  34.9 2.4 collective-permute-done.5
  41.3 1.9 convolution_bitcast_fusion.1
  45.6 1.8 collective-permute-start.6
  49.3 2.4 collective-permute-done.6
  62.2 5.7 collective-permute-start.9
  68.0 242.1 %all-reduce.12.cloned.1.call-done = f32[3,3,64,64]{3,2,1,0:T(8,128)} async-done(((f32[3,3,64,64]{3,2,1,0:T(8,128)}), f32[3,3,64,64]{3,2,1,0:T(8,128)}) %all-reduce.12.cloned.1.call-update) | async-done | bytes 147472 | tf_op jit(solution)/shard_map/psum | solution.py:109
  310.0 1.7 broadcast_multiply_fusion
  312.7 1.8 fusion.81
  314.5 1.9 fusion.83
  316.4 1.9 fusion.96
  318.3 1.9 fusion.98
  320.2 1.8 fusion.32
  322.0 2.0 fusion.37
  323.9 1.8 fusion.27
  325.8 2.3 convolution_bitcast_fusion
  328.1 2.3 convolution_bitcast_fusion.2
  331.1 6.7 %fusion.24 = bf16[1,64,4,8,256]{4,1,3,2,0:T(8,128)(2,1)S(1)} fusion(f32[4,8,256,64]{2,3,1,0:T(8,128)} %fusion.27, f32[4,8,256,64]{2,3,1,0:T(8,128)} %fusion.81, f32[4,8,256,64]{2,3,1,0:T(8,128)} %fusion.83, f32[4,8,256,64]{2,3,1,0:T(8,128)S(1)} %fusion.94, f32[4,8,256,64]{2,3,1,0:T(8,128)} %fusion.96, f32[4,8,256,64]{2,3,1,0:T(8,128)} %fusion.37, ...), kind=kOutput, calls=%fused_computation.42 | convolution fusion | flops 75497472 | bytes 19021824 | tf_op jit(solution)/shard_map/oc,bofhw->bcfhw/dot_general | solution.py:47
  337.9 1.6 copy.42
  339.4 236.0 %all-reduce.14.cloned.1.call-done = (f32[3,64,64]{2,1,0:T(8,128)}, f32[3,64,64]{2,1,0:T(8,128)}) async-done(((f32[3,64,64]{2,1,0:T(8,128)}, f32[3,64,64]{2,1,0:T(8,128)}), (f32[3,64,64]{2,1,0:T(8,128)}, f32[3,64,64]{2,1,0:T(8,128)})) %all-reduce.14.cloned.1.call-update) | async-done | bytes 98320 | tf_op jit(solution)/shard_map/psum | solution.py:109
  575.4 1.6 broadcast_multiply_fusion.1
  (87 shorter events, 33.8 us)
Async XLA Ops:
  7.2 9.1 %copy-start.1 = (bf16[1,64,4,8,256]{4,3,2,1,0:T(8,128)(2,1)S(1)}, bf16[1,64,4,8,256]{4,3,2,1,0:T(8,128)(2,1)}, u32[]{:S(2)}) copy-start(bf16[1,64,4,8,256]{4,3,2,1,0:T(8,128)(2,1)} %param.6) | copy-start | bytes 3145732
  7.2 302.8 %all-reduce.12.cloned.1.call-start = ((), (), s32[]{:S(2)}) async-start(), calls=%async_computation | async-start | bytes 589824 | tf_op jit(solution)/shard_map/psum | solution.py:109
  9.1 12.1 %collective-permute-start.2 = (bf16[1,64,4,1,256]{4,1,3,2,0:T(8,128)(2,1)S(1)}, bf16[1,64,4,1,256]{4,1,3,2,0:T(8,128)(2,1)S(1)}, u32[]{:S(2)}, u32[]{:S(2)}) collective-permute-start(bf16[1,64,4,1,256]{4,1,3,2,0:T(8,128)(2,1)S(1)} %get-tuple-element.27), channel_id=1, source_target_pairs={{0,2},{2,4},{4,6},{6,8},{8,10},{10,12},{12,14},{1,3},{3,5},{5,7},{... | collective-permute-start | bytes 393224 | tf_op jit(solution)/shard_map/ppermute | solution.py:16
  14.8 4.7 copy-start
  14.8 4.7 copy-start.5
  14.8 7.3 %collective-permute-start.3 = (bf16[1,64,4,1,256]{4,1,3,2,0:T(8,128)(2,1)S(1)}, bf16[1,64,4,1,256]{4,1,3,2,0:T(8,128)(2,1)S(1)}, u32[]{:S(2)}, u32[]{:S(2)}) collective-permute-start(bf16[1,64,4,1,256]{4,1,3,2,0:T(8,128)(2,1)S(1)} %get-tuple-element.26), channel_id=1, source_target_pairs={{2,0},{4,2},{6,4},{8,6},{10,8},{12,10},{14,12},{3,1},{5,3},{7,5},{... | collective-permute-start | bytes 393224 | tf_op jit(solution)/shard_map/ppermute | solution.py:19
  16.9 3.4 copy-start.8
  16.9 26.2 %collective-permute-start = (bf16[1,64,2,8,256]{4,1,3,2,0:T(8,128)(2,1)S(1)}, bf16[1,64,2,8,256]{4,1,3,2,0:T(8,128)(2,1)S(1)}, u32[]{:S(2)}, u32[]{:S(2)}) collective-permute-start(bf16[1,64,2,8,256]{4,1,3,2,0:T(8,128)(2,1)S(1)} %get-tuple-element.23), channel_id=1, source_target_pairs={{16,0},{32,16},{48,32},{64,48},{80,64},{96,80},{112,96},{128,112},... | collective-permute-start | bytes 1572872 | tf_op jit(solution)/shard_map/ppermute | solution.py:19
  17.9 25.7 %collective-permute-start.1 = (bf16[1,64,2,8,256]{4,1,3,2,0:T(8,128)(2,1)S(1)}, bf16[1,64,2,8,256]{4,1,3,2,0:T(8,128)(2,1)S(1)}, u32[]{:S(2)}, u32[]{:S(2)}) collective-permute-start(bf16[1,64,2,8,256]{4,1,3,2,0:T(8,128)(2,1)S(1)} %get-tuple-element.22), channel_id=1, source_target_pairs={{0,16},{16,32},{32,48},{48,64},{64,80},{80,96},{96,112},{112,128},... | collective-permute-start | bytes 1572872 | tf_op jit(solution)/shard_map/ppermute | solution.py:16
  26.0 5.1 copy-start.6
  27.5 7.0 %collective-permute-start.4 = (bf16[1,64,1,8,256]{4,1,3,2,0:T(8,128)(2,1)S(1)}, bf16[1,64,1,8,256]{4,1,3,2,0:T(8,128)(2,1)S(1)}, u32[]{:S(2)}, u32[]{:S(2)}) collective-permute-start(bf16[1,64,1,8,256]{4,1,3,2,0:T(8,128)(2,1)S(1)} %get-tuple-element.25), channel_id=1, source_target_pairs={{0,16},{16,32},{32,48},{48,64},{64,80},{80,96},{96,112},{112,128},... | collective-permute-start | bytes 786440 | tf_op jit(solution)/shard_map/ppermute | solution.py:16
  31.2 6.1 %collective-permute-start.5 = (bf16[1,64,1,8,256]{4,1,3,2,0:T(8,128)(2,1)S(1)}, bf16[1,64,1,8,256]{4,1,3,2,0:T(8,128)(2,1)S(1)}, u32[]{:S(2)}, u32[]{:S(2)}) collective-permute-start(bf16[1,64,1,8,256]{4,1,3,2,0:T(8,128)(2,1)S(1)} %get-tuple-element.24), channel_id=1, source_target_pairs={{16,0},{32,16},{48,32},{64,48},{80,64},{96,80},{112,96},{128,112},... | collective-permute-start | bytes 786440 | tf_op jit(solution)/shard_map/ppermute | solution.py:19
  38.3 4.9 copy-start.3
  39.5 286.2 %collective-permute-start.11 = (bf16[1,64,2,8,256]{4,1,3,2,0:T(8,128)(2,1)}, bf16[1,64,2,8,256]{4,1,3,2,0:T(8,128)(2,1)}, u32[]{:S(2)}, u32[]{:S(2)}) collective-permute-start(bf16[1,64,2,8,256]{4,1,3,2,0:T(8,128)(2,1)} %get-tuple-element.13), channel_id=1, source_target_pairs={{16,0},{32,16},{48,32},{64,48},{80,64},{96,80},{112,96},{128,112},... | collective-permute-start | bytes 1572872 | tf_op jit(solution)/shard_map/ppermute | solution.py:19
  40.5 287.6 %collective-permute-start.10 = (bf16[1,64,2,8,256]{4,1,3,2,0:T(8,128)(2,1)}, bf16[1,64,2,8,256]{4,1,3,2,0:T(8,128)(2,1)}, u32[]{:S(2)}, u32[]{:S(2)}) collective-permute-start(bf16[1,64,2,8,256]{4,1,3,2,0:T(8,128)(2,1)} %get-tuple-element.12), channel_id=1, source_target_pairs={{0,16},{16,32},{32,48},{48,64},{64,80},{80,96},{96,112},{112,128},... | collective-permute-start | bytes 1572872 | tf_op jit(solution)/shard_map/ppermute | solution.py:16
  45.6 6.2 %collective-permute-start.6 = (bf16[1,64,1,8,256]{4,1,3,2,0:T(8,128)(2,1)S(1)}, bf16[1,64,1,8,256]{4,1,3,2,0:T(8,128)(2,1)S(1)}, u32[]{:S(2)}, u32[]{:S(2)}) collective-permute-start(bf16[1,64,1,8,256]{4,1,3,2,0:T(8,128)(2,1)S(1)} %get-tuple-element.21), channel_id=1, source_target_pairs={{16,0},{32,16},{48,32},{64,48},{80,64},{96,80},{112,96},{128,112},... | collective-permute-start | bytes 786440 | tf_op jit(solution)/shard_map/ppermute | solution.py:19
  47.3 4.9 collective-permute-start.7
  60.2 515.2 %all-reduce.14.cloned.1.call-start = ((), (), s32[]{:S(2)}) async-start(), calls=%async_computation.1 | async-start | bytes 393216 | tf_op jit(solution)/shard_map/psum | solution.py:109
  60.9 250.8 %collective-permute-start.8 = (bf16[1,64,4,1,256]{4,1,3,2,0:T(8,128)(2,1)}, bf16[1,64,4,1,256]{4,1,3,2,0:T(8,128)(2,1)S(1)}, u32[]{:S(2)}, u32[]{:S(2)}) collective-permute-start(bf16[1,64,4,1,256]{4,1,3,2,0:T(8,128)(2,1)} %get-tuple-element.18), channel_id=1, source_target_pairs={{2,0},{4,2},{6,4},{8,6},{10,8},{12,10},{14,12},{3,1},{5,3},{7,5},{... | collective-permute-start | bytes 393224 | tf_op jit(solution)/shard_map/ppermute | solution.py:19
  62.2 249.5 %collective-permute-start.9 = (bf16[1,64,4,1,256]{4,1,3,2,0:T(8,128)(2,1)}, bf16[1,64,4,1,256]{4,1,3,2,0:T(8,128)(2,1)S(1)}, u32[]{:S(2)}, u32[]{:S(2)}) collective-permute-start(bf16[1,64,4,1,256]{4,1,3,2,0:T(8,128)(2,1)} %get-tuple-element.19), channel_id=1, source_target_pairs={{0,2},{2,4},{4,6},{6,8},{8,10},{10,12},{12,14},{1,3},{3,5},{5,7},{... | collective-permute-start | bytes 393224 | tf_op jit(solution)/shard_map/ppermute | solution.py:16
  323.9 1.8 copy-start.2
  323.9 1.9 copy-start.4
  328.1 2.3 copy-start.7
Sparse Core Ops, SparseCore 0:
  60.3 249.6 all-reduce.11
  331.3 244.0 all-reduce.13
where the time goes:
time: 584 us
  waiting for transfers between devices  486 us (83%)
  matrix products  45.6 us (8%)
  starting transfers between devices  23.8 us (4%)
  between operations  14.5 us (2%)
  local copies, waits for them, and re-layouts  7.55 us (1%)
  other arithmetic  6.37 us (1%)
    psum x2, waiting for transfers between devices, per_device(): lax.psum((grad_spatial, grad_first, grad_second), ('tm', 'height', 'batch'))  478 us
    dot_general x15, matrix products, back(): jnp.einsum('oc,bofhw->bcfhw', weight, value, preferred_element_type=jnp.f...  25.2 us
    ppermute x6, starting transfers between devices, extended(): lax.ppermute(lax.slice_in_dim(block, block.shape[dim] - width, None, axis...  17.4 us
    dot_general x15, matrix products, outer(): jnp.einsum('bofhw,bcfhw->oc', grads, value, preferred_element_type=jnp.fl...  13.2 us
  transfers between devices with their start and end apart: 14, of which 6 were waited for; matrix products, arithmetic and copies ran while one was open for 9% of the time, Pallas kernels for 0%

commit v1 on v0

v1 whole, which is shorter than its diff:
```python
import functools
import math

import jax
import jax.numpy as jnp
from jax import lax
from jax.experimental import pallas as pl
from jax.experimental.pallas import tpu as pltpu
from jax.sharding import PartitionSpec as P

BF16 = jnp.bfloat16
F32 = jnp.float32
MESH = pl.DeviceIdType.MESH
CH = 64
AXES = ("tm", "height", "batch")


def dot(left, right):
    return jnp.dot(left, right, preferred_element_type=F32)


def dot_nt(left, right):
    return lax.dot_general(left, right, (((1,), (1,)), ((), ())), preferred_element_type=F32)


def gate(value):
    t = jnp.tanh(0.5 * value)
    g = 0.6 + 0.4 * t
    return value * g, g + 0.2 * value * (1.0 - t * t)


def kernel(
    sizes, scale,
    feat, cot, ws, w1, w2,
    out, gs, g1, g2,
    raw_f, raw_c, raw_o, X, FI, D1, CT, S2, SE, BS, BF, BFL, BFR, IG,
    WF, WB, W1F, W1B, W2B, PIN, POUT,
    acc1, acc2, acc3, pack1, pack2,
    a1s, a1r, b1r, c1r, a2s, a2r, b2r, c2r,
    sem_in, sem_out, xs, xr, cs, cr, fs, fr, bs, br, rs, rr, ars, arr,
):
    ntm, nheight, nbatch = sizes
    nxy = nheight * nbatch
    nf, nr, width = raw_f.shape[0], raw_f.shape[2], raw_f.shape[3]
    t = lax.axis_index("tm")
    hh = lax.axis_index("height")
    b = lax.axis_index("batch")
    me = hh * nbatch + b
    before = (lax.rem(t + ntm - 1, ntm), hh, b)
    after = (lax.rem(t + 1, ntm), hh, b)
    above = (t, hh - 1, b)
    below = (t, hh + 1, b)
    has_above = hh > 0
    has_below = hh < nheight - 1

    def xy_device(g):
        return (t, g // nbatch, lax.rem(g, nbatch))

    def tm_device(s):
        return (s, hh, b)

    barrier = pltpu.get_barrier_semaphore()

    def greet_xy(d, _):
        pl.semaphore_signal(barrier, inc=1, device_id=xy_device(lax.rem(me + d, nxy)), device_id_type=MESH)
        return 0

    def greet_tm(d, _):
        pl.semaphore_signal(barrier, inc=1, device_id=tm_device(lax.rem(t + d, ntm)), device_id_type=MESH)
        return 0

    loads_f = [pltpu.make_async_copy(feat.at[:, f], raw_f.at[f], sem_in.at[f]) for f in range(nf)]
    loads_c = [pltpu.make_async_copy(cot.at[:, f], raw_c.at[f], sem_in.at[nf + f]) for f in range(nf)]
    for copy in loads_f + loads_c:
        copy.start()
    lax.fori_loop(1, nxy, greet_xy, 0)
    lax.fori_loop(1, ntm, greet_tm, 0)

    row = lax.broadcasted_iota(jnp.int32, (CH, 3 * CH), 0)
    col = lax.broadcasted_iota(jnp.int32, (CH, 3 * CH), 1)
    place = [jnp.where(col == row + CH * i, 1.0, 0.0).astype(BF16) for i in range(3)]
    eye = jnp.where(row[:, :CH] == col[:, :CH], 1.0, 0.0).astype(BF16)
    half = CH // 2
    prow = lax.broadcasted_iota(jnp.int32, (half * nr, half * nr), 0)
    pcol = lax.broadcasted_iota(jnp.int32, (half * nr, half * nr), 1)
    PIN[...] = jnp.where(pcol == lax.rem(prow, half) * nr + prow // half, 1.0, 0.0).astype(BF16)
    POUT[...] = jnp.where(prow == lax.rem(pcol, half) * nr + pcol // half, 1.0, 0.0).astype(BF16)
    for j in range(3):
        ahead = dot(ws[0, j], place[0]) + dot(ws[1, j], place[1]) + dot(ws[2, j], place[2])
        WF[pl.ds(CH * j, CH), :] = ahead.astype(BF16)
        turned = dot_nt(eye, jnp.concatenate([ws[2, j], ws[1, j], ws[0, j]], axis=0))
        WB[pl.ds(CH * j, CH), :] = turned.astype(BF16)
    W1F[...] = (dot(w1[0], place[0]) + dot(w1[1], place[1]) + dot(w1[2], place[2])).astype(BF16)
    W1B[...] = dot_nt(eye, jnp.concatenate([w1[2], w1[1], w1[0]], axis=0)).astype(BF16)
    W2B[...] = dot_nt(eye, jnp.concatenate([w2[2], w2[1], w2[0]], axis=0)).astype(BF16)

    edge = jnp.zeros((nf, CH, width), BF16)

    @pl.when(jnp.logical_not(has_above))
    def _():
        X[:, 0] = edge
        BF[:, 0] = edge

    @pl.when(jnp.logical_not(has_below))
    def _():
        X[:, nr + 1] = edge
        BF[:, nr + 1] = edge

    lane = lax.broadcasted_iota(jnp.int32, (CH, width), 1)

    def from_left(value):
        return jnp.where(lane == 0, 0.0, pltpu.roll(value, 1, 1))

    def from_right(value):
        return jnp.where(lane == width - 1, 0.0, pltpu.roll(value, width - 1, 1))

    def to_rows(raw, part):
        block = raw[pl.ds(half * part, half)].astype(F32).reshape(half * nr, width).astype(BF16)
        return dot(PIN[...], block).astype(BF16).reshape(nr, half, width)

    for f in range(nf):
        loads_f[f].wait()
        for part in range(2):
            X[f, pl.ds(1, nr), pl.ds(half * part, half), :] = to_rows(raw_f.at[f], part)

    pl.semaphore_wait(barrier, nxy - 1 + ntm - 1)

    def remote(src, dst, send, recv, device):
        return pltpu.make_async_remote_copy(
            src_ref=src, dst_ref=dst, send_sem=send, recv_sem=recv, device_id=device, device_id_type=MESH
        )

    x_up = remote(X.at[:, 1], X.at[:, nr + 1], xs.at[0], xr.at[0], above)
    x_down = remote(X.at[:, nr], X.at[:, 0], xs.at[1], xr.at[1], below)

    @pl.when(has_above)
    def _():
        x_up.start()

    @pl.when(has_below)
    def _():
        x_down.start()

    for f in range(nf):
        loads_c[f].wait()
        for part in range(2):
            CT[:, f % 2, f // 2 + 1, pl.ds(half * part, half), :] = to_rows(raw_c.at[f], part)
    c_back = remote(CT.at[:, :, 1], CT.at[:, :, 3], cs.at[0], cr.at[0], before)
    c_fore = remote(CT.at[:, :, 2], CT.at[:, :, 0], cs.at[1], cr.at[1], after)
    c_back.start()
    c_fore.start()

    def conv_row(f, h):
        z = dot(WF[...], X[f, pl.ds(h, 3)].reshape(3 * CH, width))
        value = z[CH : 2 * CH] + from_left(z[:CH]) + from_right(z[2 * CH :])
        act, der = gate(value)
        FI[h, f + 1] = act.astype(BF16)
        D1[f, h] = der

    def conv_inner(f, _):
        for h in range(1, nr - 1):
            conv_row(f, h)
        return 0

    lax.fori_loop(0, nf, conv_inner, 0)

    @pl.when(has_above)
    def _():
        x_up.wait_send()
        x_down.wait_recv()

    @pl.when(has_below)
    def _():
        x_down.wait_send()
        x_up.wait_recv()

    for f in (0, nf - 1):
        conv_row(f, 0)
        conv_row(f, nr - 1)
    f_back = remote(FI.at[:, 1], FI.at[:, nf + 1], fs.at[0], fr.at[0], before)
    f_fore = remote(FI.at[:, nf], FI.at[:, 0], fs.at[1], fr.at[1], after)
    f_back.start()
    f_fore.start()
    for f in range(1, nf - 1):
        conv_row(f, 0)
        conv_row(f, nr - 1)

    c_back.wait_send()
    c_fore.wait_send()
    c_back.wait_recv()
    c_fore.wait_recv()

    def back_two(h, _):
        for p in range(2):
            for q in range(2):
                S2[h, p, q] = dot(W2B[...], CT[h, p, pl.ds(q, 3)].reshape(3 * CH, width))
        return 0

    lax.fori_loop(0, nr, back_two, 0)

    def second_frame(f, h):
        value = dot(W1F[...], FI[h, pl.ds(f, 3)].reshape(3 * CH, width))
        act, der = gate(value)
        SE[h, f % 2, f // 2] = act.astype(BF16)
        BS[h, f + 1] = (S2[h, f % 2, f // 2] * der).astype(BF16)

    def second_inner(h, _):
        for f in range(1, nf - 1):
            second_frame(f, h)
        return 0

    def second_outer(h, _):
        second_frame(0, h)
        second_frame(nf - 1, h)
        return 0

    lax.fori_loop(0, nr, second_inner, 0)
    f_back.wait_send()
    f_fore.wait_send()
    f_back.wait_recv()
    f_fore.wait_recv()
    lax.fori_loop(0, nr, second_outer, 0)
    b_back = remote(BS.at[:, 1], BS.at[:, nf + 1], bs.at[0], br.at[0], before)
    b_fore = remote(BS.at[:, nf], BS.at[:, 0], bs.at[1], br.at[1], after)
    b_back.start()
    b_fore.start()

    acc1[...] = jnp.zeros_like(acc1)
    acc2[...] = jnp.zeros_like(acc2)

    def temporal_grads(h, _):
        total1 = acc1[...]
        total2 = acc2[...]
        for f in range(0, nf, 2):
            total1 += dot_nt(
                BS[h, pl.ds(f + 1, 2)].reshape(2 * CH, width), FI[h, pl.ds(f, 4)].reshape(4 * CH, width)
            )
        for p in range(2):
            total2 += dot_nt(CT[h, p].reshape(4 * CH, width), SE[h, p].reshape(2 * CH, width))
        acc1[...] = total1
        acc2[...] = total2
        return 0

    lax.fori_loop(0, nr, temporal_grads, 0)

    low = lax.broadcasted_iota(jnp.int32, (CH, 2 * CH), 1) < CH

    def side_by_side(left, right):
        return jnp.where(low[: left.shape[0]], left, pltpu.roll(right, CH, 1))

    def reduce_scatter(pack, send, recv, which):
        rows = send.shape[1]
        for g in range(nxy):
            send[g] = pack[pl.ds(rows * g, rows), :]
        recv[me] = send[me]

        def one(d, _):
            g = lax.rem(me + d, nxy)
            remote(send.at[g], recv.at[me], ars.at[which], arr.at[which], xy_device(g)).start()
            return 0

        lax.fori_loop(1, nxy, one, 0)

    def await_all(ref, count, sem):
        part = ref.at[pl.ds(0, count)]
        pltpu.make_async_copy(part, part, sem).wait()

    def added(ref):
        total = ref[0]
        for g in range(1, ref.shape[0]):
            total += ref[g]
        return total

    def exchange_tm(send, recv, spread, which):
        await_all(recv, nxy - 1, arr.at[which])
        await_all(send, nxy - 1, ars.at[which])
        spread[t] = added(recv)

        def one(d, _):
            s = lax.rem(t + d, ntm)
            remote(spread.at[t], spread.at[t], ars.at[which + 1], arr.at[which + 1], tm_device(s)).start()
            return 0

        lax.fori_loop(1, ntm, one, 0)

    def gather_xy(spread, gathered, which):
        await_all(spread, ntm - 1, arr.at[which + 1])
        await_all(spread, ntm - 1, ars.at[which + 1])
        gathered[me] = added(spread)

        def one(d, _):
            g = lax.rem(me + d, nxy)
            remote(gathered.at[me], gathered.at[me], ars.at[which + 2], arr.at[which + 2], xy_device(g)).start()
            return 0

        lax.fori_loop(1, nxy, one, 0)

    def unpack(pack, gathered, which):
        await_all(gathered, nxy - 1, arr.at[which + 2])
        await_all(gathered, nxy - 1, ars.at[which + 2])
        rows = gathered.shape[1]
        for g in range(nxy):
            pack[pl.ds(rows * g, rows), :] = gathered[g] * scale

    s1 = acc1[pl.ds(0, CH), :] + pltpu.roll(acc1[pl.ds(CH, CH), :], 3 * CH, 1)
    s2 = acc2[pl.ds(0, 3 * CH), :] + pltpu.roll(acc2[pl.ds(CH, 3 * CH), :], CH, 1)
    pack1[pl.ds(0, CH), :] = s1[:, : 2 * CH]
    pack1[pl.ds(CH, CH), :] = side_by_side(s1[:, 2 * CH :], s2[:CH])
    pack1[pl.ds(2 * CH, CH), :] = side_by_side(s2[CH : 2 * CH], s2[2 * CH :])
    reduce_scatter(pack1, a1s, a1r, 0)

    def back_frame(f, h):
        value = dot(W1B[...], BS[h, pl.ds(f, 3)].reshape(3 * CH, width)) * D1[f, h]
        BF[f, h + 1] = value.astype(BF16)
        BFL[f, h] = from_right(value).astype(BF16)
        BFR[f, h] = from_left(value).astype(BF16)

    def back_inner(h, _):
        for f in range(1, nf - 1):
            back_frame(f, h)
        return 0

    def back_outer(h, _):
        back_frame(0, h)
        back_frame(nf - 1, h)
        return 0

    ups = [
        remote(BF.at[f, 1], BF.at[f, nr + 1], rs.at[f], rr.at[f], above) for f in range(nf)
    ]
    downs = [
        remote(BF.at[f, nr], BF.at[f, 0], rs.at[nf + f], rr.at[nf + f], below) for f in range(nf)
    ]

    def send_rows(frames):
        @pl.when(has_above)
        def _():
            for f in frames:
                ups[f].start()

        @pl.when(has_below)
        def _():
            for f in frames:
                downs[f].start()

    lax.fori_loop(0, nr, back_inner, 0)
    send_rows(range(1, nf - 1))
    b_back.wait_send()
    b_fore.wait_send()
    b_back.wait_recv()
    b_fore.wait_recv()
    lax.fori_loop(0, nr, back_outer, 0)
    send_rows((0, nf - 1))

    exchange_tm(a1s, a1r, b1r, 0)

    acc3[...] = jnp.zeros_like(acc3)

    def spatial_grads(f, _):
        for h in range(0, nr, 2):
            left = jnp.concatenate(
                [
                    BFL[f, pl.ds(h, 2)].reshape(2 * CH, width),
                    BF[f, pl.ds(h + 1, 2)].reshape(2 * CH, width),
                    BFR[f, pl.ds(h, 2)].reshape(2 * CH, width),
                ],
                axis=0,
            )
            acc3[...] += dot_nt(left, X[f, pl.ds(h, 4)].reshape(4 * CH, width))
        return 0

    lax.fori_loop(0, nf, spatial_grads, 0)
    tails = []
    for j in range(3):
        total = acc3[pl.ds(2 * CH * j, CH), :] + pltpu.roll(acc3[pl.ds(2 * CH * j + CH, CH), :], 3 * CH, 1)
        pack2[pl.ds(CH * j, CH), :] = total[:, : 2 * CH]
        tails.append(total[:, 2 * CH :])
    pack2[pl.ds(3 * CH, CH), :] = side_by_side(tails[0], tails[1])
    pack2[pl.ds(4 * CH, half), :] = side_by_side(tails[2][:half], tails[2][half:])
    reduce_scatter(pack2, a2s, a2r, 3)
    gather_xy(b1r, c1r, 0)

    def grad_row(f, h):
        z = dot(WB[...], BF[f, pl.ds(h, 3)].reshape(3 * CH, width))
        value = z[CH : 2 * CH] + from_right(z[:CH]) + from_left(z[2 * CH :])
        IG[f, h] = value.astype(BF16)

    def grad_inner(f, _):
        for h in range(1, nr - 1):
            grad_row(f, h)
        return 0

    lax.fori_loop(0, nf, grad_inner, 0)
    exchange_tm(a2s, a2r, b2r, 3)

    @pl.when(has_above)
    def _():
        for f in range(nf):
            ups[f].wait_send()
            downs[f].wait_recv()

    @pl.when(has_below)
    def _():
        for f in range(nf):
            downs[f].wait_send()
            ups[f].wait_recv()

    stores = [pltpu.make_async_copy(raw_o.at[f], out.at[:, f], sem_out.at[f]) for f in range(nf)]
    for f in range(nf):
        grad_row(f, 0)
        grad_row(f, nr - 1)
        for part in range(2):
            block = IG[f, :, pl.ds(half * part, half), :].reshape(half * nr, width)
            raw_o[f, pl.ds(half * part, half)] = dot(POUT[...], block).reshape(half, nr, width).astype(BF16)
        stores[f].start()

    gather_xy(b2r, c2r, 3)

    unpack(pack1, c1r, 0)
    g1[0] = pack1[pl.ds(0, CH), :CH]
    g1[1] = pack1[pl.ds(0, CH), CH:]
    g1[2] = pack1[pl.ds(CH, CH), :CH]
    g2[2] = pack1[pl.ds(CH, CH), CH:]
    g2[1] = pack1[pl.ds(2 * CH, CH), :CH]
    g2[0] = pack1[pl.ds(2 * CH, CH), CH:]
    unpack(pack2, c2r, 3)
    for j in range(3):
        gs[0, j] = pack2[pl.ds(CH * j, CH), :CH]
        gs[1, j] = pack2[pl.ds(CH * j, CH), CH:]
    gs[2, 0] = pack2[pl.ds(3 * CH, CH), :CH]
    gs[2, 1] = pack2[pl.ds(3 * CH, CH), CH:]
    gs[2, 2, pl.ds(0, half), :] = pack2[pl.ds(4 * CH, half), :CH]
    gs[2, 2, pl.ds(half, half), :] = pack2[pl.ds(4 * CH, half), CH:]
    for f in range(nf):
        stores[f].wait()


def per_device(sizes, features, cotangent, w_spatial, w_first, w_second):
    _, ch, nf, nr, width = features.shape
    ntm, nheight, nbatch = sizes
    nxy = nheight * nbatch
    count = nbatch * nf * ntm * nr * nheight * width
    scale = 1.0 / math.sqrt(count)
    vmem = lambda shape, kind=BF16: pltpu.VMEM(shape, kind)
    rows1, rows2 = 3 * ch // nxy, 9 * ch // 2 // nxy
    dma = pltpu.SemaphoreType.DMA
    scratch = [
        vmem((nf, ch, nr, width)), vmem((nf, ch, nr, width)), vmem((nf, ch, nr, width)),
        vmem((nf, nr + 2, ch, width)),
        vmem((nr, nf + 2, ch, width)),
        vmem((nf, nr, ch, width), F32),
        vmem((nr, 2, nf // 2 + 2, ch, width)),
        vmem((nr, 2, nf // 2, ch, width), F32),
        vmem((nr, 2, nf // 2, ch, width)),
        vmem((nr, nf + 2, ch, width)),
        vmem((nf, nr + 2, ch, width)),
        vmem((nf, nr, ch, width)), vmem((nf, nr, ch, width)), vmem((nf, nr, ch, width)),
        vmem((3 * ch, 3 * ch)), vmem((3 * ch, 3 * ch)),
        vmem((ch, 3 * ch)), vmem((ch, 3 * ch)), vmem((ch, 3 * ch)),
        vmem((ch // 2 * nr, ch // 2 * nr)), vmem((ch // 2 * nr, ch // 2 * nr)),
        vmem((2 * ch, 4 * ch), F32), vmem((4 * ch, 2 * ch), F32), vmem((6 * ch, 4 * ch), F32),
        vmem((3 * ch, 2 * ch), F32), vmem((9 * ch // 2, 2 * ch), F32),
        vmem((nxy, rows1, 2 * ch), F32), vmem((nxy, rows1, 2 * ch), F32),
        vmem((ntm, rows1, 2 * ch), F32), vmem((nxy, rows1, 2 * ch), F32),
        vmem((nxy, rows2, 2 * ch), F32), vmem((nxy, rows2, 2 * ch), F32),
        vmem((ntm, rows2, 2 * ch), F32), vmem((nxy, rows2, 2 * ch), F32),
        dma((2 * nf,)), dma((nf,)),
        dma((2,)), dma((2,)), dma((2,)), dma((2,)), dma((2,)), dma((2,)), dma((2,)), dma((2,)),
        dma((2 * nf,)), dma((2 * nf,)), dma((6,)), dma((6,)),
    ]
    here = pl.BlockSpec(memory_space=pltpu.VMEM)
    anywhere = pl.BlockSpec(memory_space=pl.ANY)
    input_grad, grad_spatial, grad_first, grad_second = pl.pallas_call(
        functools.partial(kernel, sizes, scale),
        out_shape=(
            jax.ShapeDtypeStruct((ch, nf, nr, width), BF16),
            jax.ShapeDtypeStruct((3, 3, ch, ch), F32),
            jax.ShapeDtypeStruct((3, ch, ch), F32),
            jax.ShapeDtypeStruct((3, ch, ch), F32),
        ),
        in_specs=[anywhere, anywhere, here, here, here],
        out_specs=(anywhere, here, here, here),
        scratch_shapes=scratch,
        compiler_params=pltpu.CompilerParams(
            collective_id=0, has_side_effects=True, vmem_limit_bytes=48 * 1024 * 1024
        ),
        name="critic_step",
    )(features[0], cotangent[0], w_spatial, w_first, w_second)
    return input_grad[None], grad_spatial, grad_first, grad_second


def solution(mesh):
    sizes = tuple(mesh.shape[axis] for axis in AXES)
    big = P("batch", None, "tm", "height", None)
    return jax.shard_map(
        functools.partial(per_device, sizes),
        mesh=mesh,
        in_specs=(big, big, P(), P(), P()),
        out_specs=(big, P(), P(), P()),
        check_vma=False,
    )
```

time: 584 us -> 62.4 us (0.11)
  waiting for transfers between devices: 486 us -> 0 us
  Pallas kernels: 0 us -> 53.5 us
  matrix products: 45.6 us -> 0 us
  starting transfers between devices: 23.8 us -> 0 us
  between operations: 14.5 us -> 0.65 us
  other arithmetic: 6.37 us -> 0 us
    psum x2 -> x0, waiting for transfers between devices: 478 us -> none  [per_device(): lax.psum((grad_spatial, grad_first, grad_second), ('tm', 'height', 'batch'))]
    pallas_call x0 -> x1, Pallas kernels: none -> 53.5 us  [per_device(): pl.pallas_call(functools.partial(kernel, sizes, scale), out_shape=(jax.Sh...]
    dot_general x42 -> x0, matrix products: 45.6 us -> none  [the longest x15 25.2 us: back(): jnp.einsum('oc,bofhw->bcfhw', weight, value, preferred_element_type=jnp.f...]
    ppermute x12 -> x0, starting transfers between devices: 23.8 us -> none  [the longest x6 17.4 us: extended(): lax.ppermute(lax.slice_in_dim(block, block.shape[dim] - width, None, axis...]
    ppermute x12 -> x0, waiting for transfers between devices: 8.03 us -> none  [the longest x6 5.11 us: extended(): lax.ppermute(lax.slice_in_dim(block, 0, width, axis=dim), axis, backward)]
  transfers between devices with their start and end apart: 14 -> 0, of which waited for: 6 -> 0; matrix products, arithmetic and copies ran while one was open for 9% -> 0% of each run, Pallas kernels for 0% -> 0%
where the time goes in v1:
time: 62.4 us; the launch traced here: 62.1 us
  Pallas kernels  53.5 us (86%)
  local copies, waits for them, and re-layouts  7.91 us (13%)
  between operations  0.65 us (1%)
    pallas_call x1, Pallas kernels, per_device(): pl.pallas_call(functools.partial(kernel, sizes, scale), out_shape=(jax.Sh...  53.5 us
    unnamed x14, local copies, waits for them, and re-layouts  7.91 us

profile of v1, /device:TPU:1, one launch (start us, length us, event | category | flops | bytes accessed | tf_op | source)
XLA Modules:
  0.0 62.1 jit_solution(9168008910210630613)
XLA Ops:
  0.6 0.0 copy-start
  0.6 1.2 %copy-done = bf16[1,64,4,8,256]{4,3,2,1,0:T(8,128)(2,1)S(1)} copy-done((bf16[1,64,4,8,256]{4,3,2,1,0:T(8,128)(2,1)S(1)}, bf16[1,64,4,8,256]{4,3,2,1,0:T(8,128)(2,1)}, u32[]{:S(2)}) %copy-start) | copy-done | bytes 1048600
  1.9 0.0 copy-start.1
  1.9 1.2 %copy-done.1 = bf16[1,64,4,8,256]{4,3,2,1,0:T(8,128)(2,1)S(1)} copy-done((bf16[1,64,4,8,256]{4,3,2,1,0:T(8,128)(2,1)S(1)}, bf16[1,64,4,8,256]{4,3,2,1,0:T(8,128)(2,1)}, u32[]{:S(2)}) %copy-start.1) | copy-done | bytes 1048600
  3.1 0.0 copy-start.2
  3.1 0.9 %copy-done.2 = bf16[3,3,64,64]{3,2,1,0:T(8,128)(2,1)S(1)} copy-done((bf16[3,3,64,64]{3,2,1,0:T(8,128)(2,1)S(1)}, bf16[3,3,64,64]{3,2,1,0:T(8,128)(2,1)}, u32[]{:S(2)}) %copy-start.2) | copy-done | bytes 73752
  4.0 0.0 copy-start.3
  4.0 0.8 %copy-done.3 = bf16[3,64,64]{2,1,0:T(8,128)(2,1)S(1)} copy-done((bf16[3,64,64]{2,1,0:T(8,128)(2,1)S(1)}, bf16[3,64,64]{2,1,0:T(8,128)(2,1)}, u32[]{:S(2)}) %copy-start.3) | copy-done | bytes 24600
  4.8 0.0 copy-start.4
  4.8 0.8 %copy-done.4 = bf16[3,64,64]{2,1,0:T(8,128)(2,1)S(1)} copy-done((bf16[3,64,64]{2,1,0:T(8,128)(2,1)S(1)}, bf16[3,64,64]{2,1,0:T(8,128)(2,1)}, u32[]{:S(2)}) %copy-start.4) | copy-done | bytes 24600
  5.6 53.5 %critic_step.1 = (bf16[64,4,8,256]{3,2,1,0:T(8,128)(2,1)S(1)}, f32[3,3,64,64]{3,2,1,0:T(8,128)S(1)}, f32[3,64,64]{2,1,0:T(8,128)S(1)}, f32[3,64,64]{2,1,0:T(8,128)S(1)}) custom-call(bf16[64,4,8,256]{3,2,1,0:T(8,128)(2,1)S(1)} %bitcast.3, bf16[64,4,8,256]{3,2,1,0:T(8,128)(2,1)S(1)} %bitcast.4, bf16[3,3,64,64]{3,2,1,0:T(8,128)(2,1)S(1)} %copy-done.2, ...), custom_call_target="tpu_custom_call" | custom-call | tf_op jit(solution)/shard_map/critic_step/pallas_call | solution.py:473
  59.1 1.0 %copy.13 = bf16[1,64,4,8,256]{4,3,2,1,0:T(8,128)(2,1)} copy(bf16[1,64,4,8,256]{4,3,2,1,0:T(8,128)(2,1)S(1)} %bitcast.5) | data formatting | bytes 2097152
  60.1 0.7 %copy.14 = f32[3,3,64,64]{3,2,1,0:T(8,128)} copy(f32[3,3,64,64]{3,2,1,0:T(8,128)S(1)} %get-tuple-element.17) | data formatting | bytes 294912
  60.8 0.6 %copy.15 = f32[3,64,64]{2,1,0:T(8,128)} copy(f32[3,64,64]{2,1,0:T(8,128)S(1)} %get-tuple-element.18) | data formatting | bytes 98304
  61.5 0.6 %copy.16 = f32[3,64,64]{2,1,0:T(8,128)} copy(f32[3,64,64]{2,1,0:T(8,128)S(1)} %get-tuple-element.19) | data formatting | bytes 98304
Async XLA Ops:
  0.6 1.2 %copy-start = (bf16[1,64,4,8,256]{4,3,2,1,0:T(8,128)(2,1)S(1)}, bf16[1,64,4,8,256]{4,3,2,1,0:T(8,128)(2,1)}, u32[]{:S(2)}) copy-start(bf16[1,64,4,8,256]{4,3,2,1,0:T(8,128)(2,1)} %param.5) | copy-start | bytes 3145732
  1.9 1.2 %copy-start.1 = (bf16[1,64,4,8,256]{4,3,2,1,0:T(8,128)(2,1)S(1)}, bf16[1,64,4,8,256]{4,3,2,1,0:T(8,128)(2,1)}, u32[]{:S(2)}) copy-start(bf16[1,64,4,8,256]{4,3,2,1,0:T(8,128)(2,1)} %param.6) | copy-start | bytes 3145732
  3.1 0.9 %copy-start.2 = (bf16[3,3,64,64]{3,2,1,0:T(8,128)(2,1)S(1)}, bf16[3,3,64,64]{3,2,1,0:T(8,128)(2,1)}, u32[]{:S(2)}) copy-start(bf16[3,3,64,64]{3,2,1,0:T(8,128)(2,1)} %ws.1) | copy-start | bytes 221188
  4.0 0.8 %copy-start.3 = (bf16[3,64,64]{2,1,0:T(8,128)(2,1)S(1)}, bf16[3,64,64]{2,1,0:T(8,128)(2,1)}, u32[]{:S(2)}) copy-start(bf16[3,64,64]{2,1,0:T(8,128)(2,1)} %w1.1) | copy-start | bytes 73732
  4.8 0.8 %copy-start.4 = (bf16[3,64,64]{2,1,0:T(8,128)(2,1)S(1)}, bf16[3,64,64]{2,1,0:T(8,128)(2,1)}, u32[]{:S(2)}) copy-start(bf16[3,64,64]{2,1,0:T(8,128)(2,1)} %w2.1) | copy-start | bytes 73732

commit v2 on v1

v2 whole, which is shorter than its diff:
```python
import functools
import math

import jax
import jax.numpy as jnp
from jax import lax
from jax.experimental import pallas as pl
from jax.experimental.pallas import tpu as pltpu
from jax.sharding import PartitionSpec as P

BF16 = jnp.bfloat16
F32 = jnp.float32
MESH = pl.DeviceIdType.MESH
CH = 64
AXES = ("tm", "height", "batch")


def dot(left, right):
    return jnp.dot(left, right, preferred_element_type=F32)


def dot_nt(left, right):
    return lax.dot_general(left, right, (((1,), (1,)), ((), ())), preferred_element_type=F32)


def gate(value):
    t = jnp.tanh(0.5 * value)
    g = 0.6 + 0.4 * t
    return value * g, g + 0.2 * value * (1.0 - t * t)


def finish(packed1, packed2, block, out, gs, g1, g2, gs_v, g1_v, g2_v, sems):
    big = pltpu.make_async_copy(block, out, sems.at[0])
    big.start()
    half = CH // 2
    g1_v[0] = packed1[pl.ds(0, CH), :CH]
    g1_v[1] = packed1[pl.ds(0, CH), CH:]
    g1_v[2] = packed1[pl.ds(CH, CH), :CH]
    g2_v[2] = packed1[pl.ds(CH, CH), CH:]
    g2_v[1] = packed1[pl.ds(2 * CH, CH), :CH]
    g2_v[0] = packed1[pl.ds(2 * CH, CH), CH:]
    for j in range(3):
        gs_v[0, j] = packed2[pl.ds(CH * j, CH), :CH]
        gs_v[1, j] = packed2[pl.ds(CH * j, CH), CH:]
    gs_v[2, 0] = packed2[pl.ds(3 * CH, CH), :CH]
    gs_v[2, 1] = packed2[pl.ds(3 * CH, CH), CH:]
    gs_v[2, 2, pl.ds(0, half), :] = packed2[pl.ds(4 * CH, half), :CH]
    gs_v[2, 2, pl.ds(half, half), :] = packed2[pl.ds(4 * CH, half), CH:]
    small = [
        pltpu.make_async_copy(source, target, sems.at[1 + n])
        for n, (source, target) in enumerate(((gs_v, gs), (g1_v, g1), (g2_v, g2)))
    ]
    for copy in small:
        copy.start()
    for copy in small:
        copy.wait()
    big.wait()


def kernel(
    sizes, scale,
    feat, cot, ws_hbm, w1_hbm, w2_hbm,
    raw_o, out1, out2,
    ws, w1, w2, raw_f, raw_c, X, FI, D1, D2, CT, SE, BS, BF, BFL, BFR, IG,
    WF, WB, W1F, W1B, W1F2, W1B2, W2B, PIN, POUT,
    pack1, pack2,
    a1s, a1r, b1r, c1r, a2s, a2r, b2r, c2r,
    sem_in, sends, recvs, ars, arr,
):
    ntm, nheight, nbatch = sizes
    nxy = nheight * nbatch
    nf, nr, width = raw_f.shape[0], raw_f.shape[2], raw_f.shape[3]
    last = nf - 1
    place_of = {0: 0, last: 1, 1: 2, 2: 3}
    outer, inner = (0, last), (1, 2)
    t = lax.axis_index("tm")
    hh = lax.axis_index("height")
    b = lax.axis_index("batch")
    me = hh * nbatch + b
    before = (lax.rem(t + ntm - 1, ntm), hh, b)
    after = (lax.rem(t + 1, ntm), hh, b)
    above = (t, hh - 1, b)
    below = (t, hh + 1, b)
    has_above = hh > 0
    has_below = hh < nheight - 1

    def xy_device(g):
        return (t, g // nbatch, lax.rem(g, nbatch))

    def tm_device(s):
        return (s, hh, b)

    barrier = pltpu.get_barrier_semaphore()

    def greet_xy(d, _):
        pl.semaphore_signal(barrier, inc=1, device_id=xy_device(lax.rem(me + d, nxy)), device_id_type=MESH)
        return 0

    def greet_tm(d, _):
        pl.semaphore_signal(barrier, inc=1, device_id=tm_device(lax.rem(t + d, ntm)), device_id_type=MESH)
        return 0

    loads_w = [
        pltpu.make_async_copy(source, target, sem_in.at[2 * nf + n])
        for n, (source, target) in enumerate(((ws_hbm, ws), (w1_hbm, w1), (w2_hbm, w2)))
    ]
    loads_f = [pltpu.make_async_copy(feat.at[:, f], raw_f.at[f], sem_in.at[f]) for f in range(nf)]
    loads_c = [pltpu.make_async_copy(cot.at[:, f], raw_c.at[f], sem_in.at[nf + f]) for f in range(nf)]
    for copy in loads_w + loads_f + loads_c:
        copy.start()
    lax.fori_loop(1, nxy, greet_xy, 0)
    lax.fori_loop(1, ntm, greet_tm, 0)

    row = lax.broadcasted_iota(jnp.int32, (CH, 4 * CH), 0)
    col = lax.broadcasted_iota(jnp.int32, (CH, 4 * CH), 1)
    place = [jnp.where(col == row + CH * i, 1.0, 0.0).astype(BF16) for i in range(4)]
    eye = place[0][:, :CH]
    half = CH // 2
    prow = lax.broadcasted_iota(jnp.int32, (half * nr, half * nr), 0)
    pcol = lax.broadcasted_iota(jnp.int32, (half * nr, half * nr), 1)
    PIN[...] = jnp.where(pcol == lax.rem(prow, half) * nr + prow // half, 1.0, 0.0).astype(BF16)
    POUT[...] = jnp.where(prow == lax.rem(pcol, half) * nr + pcol // half, 1.0, 0.0).astype(BF16)
    edge = jnp.zeros((nf, CH, width), BF16)

    @pl.when(jnp.logical_not(has_above))
    def _():
        X[:, 0] = edge
        BF[:, 0] = edge

    @pl.when(jnp.logical_not(has_below))
    def _():
        X[:, nr + 1] = edge
        BF[:, nr + 1] = edge

    def side(parts, at):
        total = dot(parts[0], place[at])
        for i in range(1, len(parts)):
            total += dot(parts[i], place[at + i])
        return total.astype(BF16)

    def turned(parts):
        return dot_nt(eye, jnp.concatenate(parts, axis=0)).astype(BF16)

    for copy in loads_w:
        copy.wait()
    for j in range(3):
        WF[pl.ds(CH * j, CH), :] = side([ws[0, j], ws[1, j], ws[2, j]], 0)[:, : 3 * CH]
        WB[pl.ds(CH * j, CH), :] = turned([ws[2, j], ws[1, j], ws[0, j]])
    none = jnp.zeros((CH, CH), BF16)
    W1F[...] = side([w1[0], w1[1], w1[2]], 0)[:, : 3 * CH]
    W1B[...] = turned([w1[2], w1[1], w1[0]])
    W2B[...] = turned([w2[2], w2[1], w2[0]])
    for a in range(2):
        W1F2[pl.ds(CH * a, CH), :] = side([w1[0], w1[1], w1[2]], a)
        W1B2[pl.ds(CH * a, CH), :] = turned([none] * a + [w1[2], w1[1], w1[0]] + [none] * (1 - a))

    lane = lax.broadcasted_iota(jnp.int32, (CH, width), 1)

    def from_left(value):
        return jnp.where(lane == 0, 0.0, pltpu.roll(value, 1, 1))

    def from_right(value):
        return jnp.where(lane == width - 1, 0.0, pltpu.roll(value, width - 1, 1))

    def to_rows(raw, part):
        block = raw[pl.ds(half * part, half)].astype(F32).reshape(half * nr, width).astype(BF16)
        return dot(PIN[...], block).astype(BF16).reshape(nr, half, width)

    def conv_row(at, f, h, s):
        z = dot(WF[...], X[at, pl.ds(h, 3)].reshape(3 * CH, width))
        value = z[CH : 2 * CH] + from_left(z[:CH]) + from_right(z[2 * CH :])
        act, der = gate(value)
        FI[s, f + 1] = act.astype(BF16)
        D1[at, h] = der

    for f in outer + inner:
        loads_f[f].wait()
        for part in range(2):
            X[place_of[f], pl.ds(1, nr), pl.ds(half * part, half), :] = to_rows(raw_f.at[f], part)
        for h in range(1, nr - 1):
            conv_row(place_of[f], f, h, h + 1)
    for f in range(nf):
        loads_c[f].wait()
        for part in range(2):
            lanes = pl.ds(half * part, half)
            block = to_rows(raw_c.at[f], part)
            CT[0, f % 2, f // 2 + 1, lanes, :] = block[0]
            CT[1, f % 2, f // 2 + 1, lanes, :] = block[nr - 1]
            CT[pl.ds(2, nr - 2), f % 2, f // 2 + 1, lanes, :] = block[1 : nr - 1]

    pl.semaphore_wait(barrier, nxy - 1 + ntm - 1)

    used = [0]

    def remote(src, dst, device):
        n = used[0]
        used[0] += 1
        return pltpu.make_async_remote_copy(
            src_ref=src, dst_ref=dst, send_sem=sends.at[n], recv_sem=recvs.at[n],
            device_id=device, device_id_type=MESH,
        )

    class Rows:
        def __init__(self, array, frames):
            self.up = remote(array.at[frames, 1], array.at[frames, nr + 1], above)
            self.down = remote(array.at[frames, nr], array.at[frames, 0], below)

        def start(self):
            pl.when(has_above)(self.up.start)
            pl.when(has_below)(self.down.start)

        def wait(self):
            @pl.when(has_above)
            def _():
                self.up.wait_send()
                self.down.wait_recv()

            @pl.when(has_below)
            def _():
                self.down.wait_send()
                self.up.wait_recv()

    class Frames:
        def __init__(self, back_src, back_dst, fore_src, fore_dst):
            self.both = (remote(back_src, back_dst, before), remote(fore_src, fore_dst, after))

        def start(self):
            for copy in self.both:
                copy.start()

        def wait(self):
            for copy in self.both:
                copy.wait_send()
                copy.wait_recv()

    def outer_frames(array, rows):
        return Frames(array.at[rows, 1], array.at[rows, nf + 1], array.at[rows, nf], array.at[rows, 0])

    edges, middle = pl.ds(0, 2), pl.ds(2, nr - 2)
    first_two, second_two = pl.ds(0, 2), pl.ds(2, 2)
    x_outer, x_inner = Rows(X, first_two), Rows(X, second_two)
    first_middle, first_edges = outer_frames(FI, middle), outer_frames(FI, edges)
    cot_far = Frames(CT.at[:, 1, 1], CT.at[:, 1, 3], CT.at[:, 0, 2], CT.at[:, 0, 0])
    cot_near = Frames(CT.at[:, 0, 1], CT.at[:, 0, 3], CT.at[:, 1, 2], CT.at[:, 1, 0])
    back_middle, back_edges = outer_frames(BS, middle), outer_frames(BS, edges)
    rows_inner, rows_outer = Rows(BF, second_two), Rows(BF, first_two)

    x_outer.start()
    first_middle.start()
    cot_far.start()
    x_inner.start()

    def keep_second(f, s, value):
        act, der = gate(value)
        SE[s, f % 2, f // 2] = act.astype(BF16)
        D2[s, f] = der

    def second_inner(s):
        z = dot(W1F2[...], FI[s, pl.ds(1, 4)].reshape(4 * CH, width))
        keep_second(1, s, z[:CH])
        keep_second(2, s, z[CH:])

    def second_outer(s):
        for f in outer:
            keep_second(f, s, dot(W1F[...], FI[s, pl.ds(f, 3)].reshape(3 * CH, width)))

    def back_second(f, s):
        p, q = f % 2, f // 2
        total = dot(W2B[...], CT[s, p, pl.ds(q, 3)].reshape(3 * CH, width))
        BS[s, f + 1] = (total * D2[s, f]).astype(BF16)

    for s in range(2, nr):
        second_inner(s)
    cot_near.start()
    first_middle.wait()
    for s in range(2, nr):
        second_outer(s)

    x_outer.wait()
    for f in outer:
        conv_row(place_of[f], f, 0, 0)
        conv_row(place_of[f], f, nr - 1, 1)
    first_edges.start()

    cot_far.wait()
    for s in range(2, nr):
        for f in outer:
            back_second(f, s)
    back_middle.start()

    x_inner.wait()
    for f in inner:
        conv_row(place_of[f], f, 0, 0)
        conv_row(place_of[f], f, nr - 1, 1)
    for s in range(2):
        second_inner(s)

    first_edges.wait()
    for s in range(2):
        second_outer(s)
        for f in outer:
            back_second(f, s)
    back_edges.start()

    cot_near.wait()
    for s in range(nr):
        for f in inner:
            back_second(f, s)

    def keep_back(f, h, value):
        at = place_of[f]
        value = value * D1[at, h]
        BF[at, h + 1] = value.astype(BF16)
        BFL[at, h] = from_right(value).astype(BF16)
        BFR[at, h] = from_left(value).astype(BF16)

    def back_inner(h, s):
        z = dot(W1B2[...], BS[s, pl.ds(1, 4)].reshape(4 * CH, width))
        keep_back(1, h, z[:CH])
        keep_back(2, h, z[CH:])

    def back_outer(h, s):
        for f in outer:
            keep_back(f, h, dot(W1B[...], BS[s, pl.ds(f, 3)].reshape(3 * CH, width)))

    back_inner(0, 0)
    back_inner(nr - 1, 1)
    rows_inner.start()
    for h in range(1, nr - 1):
        back_inner(h, h + 1)
    back_middle.wait()
    for h in range(1, nr - 1):
        back_outer(h, h + 1)

    low = lax.broadcasted_iota(jnp.int32, (CH, 2 * CH), 1) < CH

    def side_by_side(left, right):
        return jnp.where(low[: left.shape[0]], left, pltpu.roll(right, CH, 1))

    def reduce_scatter(pack, send, recv, which):
        rows = send.shape[1]
        for g in range(nxy):
            send[g] = pack[pl.ds(rows * g, rows), :]
        recv[me] = send[me]

        def one(d, _):
            g = lax.rem(me + d, nxy)
            copy_to(send.at[g], recv.at[me], which, xy_device(g)).start()
            return 0

        lax.fori_loop(1, nxy, one, 0)

    def copy_to(src, dst, which, device):
        return pltpu.make_async_remote_copy(
            src_ref=src, dst_ref=dst, send_sem=ars.at[which], recv_sem=arr.at[which],
            device_id=device, device_id_type=MESH,
        )

    def await_all(ref, count, sem):
        part = ref.at[pl.ds(0, count)]
        pltpu.make_async_copy(part, part, sem).wait()

    def added(ref):
        total = ref[0]
        for g in range(1, ref.shape[0]):
            total += ref[g]
        return total

    def exchange_tm(send, recv, spread, which):
        await_all(recv, nxy - 1, arr.at[which])
        await_all(send, nxy - 1, ars.at[which])
        spread[t] = added(recv)

        def one(d, _):
            s = lax.rem(t + d, ntm)
            copy_to(spread.at[t], spread.at[t], which + 1, tm_device(s)).start()
            return 0

        lax.fori_loop(1, ntm, one, 0)

    def gather_xy(spread, gathered, which):
        await_all(spread, ntm - 1, arr.at[which + 1])
        await_all(spread, ntm - 1, ars.at[which + 1])
        gathered[me] = added(spread)

        def one(d, _):
            g = lax.rem(me + d, nxy)
            copy_to(gathered.at[me], gathered.at[me], which + 2, xy_device(g)).start()
            return 0

        lax.fori_loop(1, nxy, one, 0)

    def unpack(packed, gathered, which):
        await_all(gathered, nxy - 1, arr.at[which + 2])
        await_all(gathered, nxy - 1, ars.at[which + 2])
        rows = gathered.shape[1]
        for g in range(nxy):
            packed[pl.ds(rows * g, rows), :] = gathered[g] * scale

    def lanes_of(parts):
        return jnp.concatenate(parts, axis=1)

    total1 = jnp.zeros((2 * CH, 4 * CH), F32)
    total2 = jnp.zeros((4 * CH, 2 * CH), F32)
    for s in range(0, nr, 2):
        at = [(s, 0), (s, 2), (s + 1, 0), (s + 1, 2)]
        total1 += dot_nt(
            lanes_of([BS[n, pl.ds(f + 1, 2)].reshape(2 * CH, width) for n, f in at]),
            lanes_of([FI[n, pl.ds(f, 4)].reshape(4 * CH, width) for n, f in at]),
        )
        at = [(s, 0), (s, 1), (s + 1, 0), (s + 1, 1)]
        total2 += dot_nt(
            lanes_of([CT[n, p].reshape(4 * CH, width) for n, p in at]),
            lanes_of([SE[n, p].reshape(2 * CH, width) for n, p in at]),
        )
    s1 = total1[:CH] + pltpu.roll(total1[CH:], 3 * CH, 1)
    s2 = total2[: 3 * CH] + pltpu.roll(total2[CH:], CH, 1)
    pack1[pl.ds(0, CH), :] = s1[:, : 2 * CH]
    pack1[pl.ds(CH, CH), :] = side_by_side(s1[:, 2 * CH :], s2[:CH])
    pack1[pl.ds(2 * CH, CH), :] = side_by_side(s2[CH : 2 * CH], s2[2 * CH :])
    reduce_scatter(pack1, a1s, a1r, 0)

    wide = [jnp.zeros((2 * CH, 4 * CH), F32)] * 3

    def versions(at, h, count):
        return (
            BFL[at, pl.ds(h, count)].reshape(count * CH, width),
            BF[at, pl.ds(h + 1, count)].reshape(count * CH, width),
            BFR[at, pl.ds(h, count)].reshape(count * CH, width),
        )

    def spatial(at_list, count):
        lefts = [versions(at, h, count) for at, h in at_list]
        right = lanes_of([X[at, pl.ds(h, count + 2)].reshape((count + 2) * CH, width) for at, h in at_list])
        left = jnp.concatenate([lanes_of([v[j] for v in lefts]) for j in range(3)], axis=0)
        return dot_nt(left, right)

    pairs = spatial([(0, h) for h in range(1, nr - 1, 2)], 2)
    for at in range(1, nf):
        pairs += spatial([(at, h) for h in range(1, nr - 1, 2)], 2)
    for j in range(3):
        total = pairs[2 * CH * j : 2 * CH * j + CH] + pltpu.roll(pairs[2 * CH * j + CH : 2 * CH * (j + 1)], 3 * CH, 1)
        wide[j] = total[:, : 3 * CH]

    back_edges.wait()
    back_outer(0, 0)
    back_outer(nr - 1, 1)
    singles = spatial([(at, h) for at in range(nf) for h in (0, nr - 1)], 1)
    tails = []
    for j in range(3):
        total = wide[j] + singles[CH * j : CH * (j + 1)]
        pack2[pl.ds(CH * j, CH), :] = total[:, : 2 * CH]
        tails.append(jnp.concatenate([total[:, 2 * CH :], total[:, 2 * CH :]], axis=1))
    pack2[pl.ds(3 * CH, CH), :] = jnp.where(low, tails[0], tails[1])
    pack2[pl.ds(4 * CH, half), :] = jnp.where(low[:half], tails[2][:half], tails[2][half:])
    reduce_scatter(pack2, a2s, a2r, 3)
    rows_outer.start()
    exchange_tm(a1s, a1r, b1r, 0)

    def grad_row(at, h):
        z = dot(WB[...], BF[at, pl.ds(h, 3)].reshape(3 * CH, width))
        value = z[CH : 2 * CH] + from_right(z[:CH]) + from_left(z[2 * CH :])
        IG[at, h] = value.astype(BF16)

    def hand_out(f):
        at = place_of[f]
        grad_row(at, 0)
        grad_row(at, nr - 1)
        for part in range(2):
            block = IG[at, :, pl.ds(half * part, half), :].reshape(half * nr, width)
            raw_o[pl.ds(half * part, half), f] = dot(POUT[...], block).reshape(half, nr, width).astype(BF16)

    def grad_inner(at, _):
        for h in range(1, nr - 1):
            grad_row(at, h)
        return 0

    lax.fori_loop(0, nf, grad_inner, 0)
    exchange_tm(a2s, a2r, b2r, 3)
    rows_inner.wait()
    for f in inner:
        hand_out(f)
    gather_xy(b1r, c1r, 0)
    rows_outer.wait()
    for f in outer:
        hand_out(f)
    gather_xy(b2r, c2r, 3)
    unpack(out1, c1r, 0)
    unpack(out2, c2r, 3)


def per_device(sizes, features, cotangent, w_spatial, w_first, w_second):
    _, ch, nf, nr, width = features.shape
    ntm, nheight, nbatch = sizes
    nxy = nheight * nbatch
    count = nbatch * nf * ntm * nr * nheight * width
    scale = 1.0 / math.sqrt(count)
    vmem = lambda shape, kind=BF16: pltpu.VMEM(shape, kind)
    all1, all2 = 3 * ch, 9 * ch // 2
    rows1, rows2 = all1 // nxy, all2 // nxy
    dma = pltpu.SemaphoreType.DMA
    scratch = [
        vmem((3, 3, ch, ch)), vmem((3, ch, ch)), vmem((3, ch, ch)),
        vmem((nf, ch, nr, width)), vmem((nf, ch, nr, width)),
        vmem((nf, nr + 2, ch, width)),
        vmem((nr, nf + 2, ch, width)),
        vmem((nf, nr, ch, width), F32),
        vmem((nr, nf, ch, width), F32),
        vmem((nr, 2, nf // 2 + 2, ch, width)),
        vmem((nr, 2, nf // 2, ch, width)),
        vmem((nr, nf + 2, ch, width)),
        vmem((nf, nr + 2, ch, width)),
        vmem((nf, nr, ch, width)), vmem((nf, nr, ch, width)), vmem((nf, nr, ch, width)),
        vmem((3 * ch, 3 * ch)), vmem((3 * ch, 3 * ch)),
        vmem((ch, 3 * ch)), vmem((ch, 3 * ch)), vmem((2 * ch, 4 * ch)), vmem((2 * ch, 4 * ch)), vmem((ch, 3 * ch)),
        vmem((ch // 2 * nr, ch // 2 * nr)), vmem((ch // 2 * nr, ch // 2 * nr)),
        vmem((all1, 2 * ch), F32), vmem((all2, 2 * ch), F32),
        vmem((nxy, rows1, 2 * ch), F32), vmem((nxy, rows1, 2 * ch), F32),
        vmem((ntm, rows1, 2 * ch), F32), vmem((nxy, rows1, 2 * ch), F32),
        vmem((nxy, rows2, 2 * ch), F32), vmem((nxy, rows2, 2 * ch), F32),
        vmem((ntm, rows2, 2 * ch), F32), vmem((nxy, rows2, 2 * ch), F32),
        dma((2 * nf + 3,)), dma((20,)), dma((20,)), dma((6,)), dma((6,)),
    ]
    here = pl.BlockSpec(memory_space=pltpu.VMEM)
    far = pl.BlockSpec(memory_space=pltpu.HBM)
    block, packed1, packed2 = pl.pallas_call(
        functools.partial(kernel, sizes, scale),
        out_shape=(
            jax.ShapeDtypeStruct((ch, nf, nr, width), BF16),
            jax.ShapeDtypeStruct((all1, 2 * ch), F32),
            jax.ShapeDtypeStruct((all2, 2 * ch), F32),
        ),
        in_specs=[far] * 5,
        out_specs=(here, here, here),
        scratch_shapes=scratch,
        compiler_params=pltpu.CompilerParams(
            collective_id=0, has_side_effects=True, vmem_limit_bytes=48 * 1024 * 1024
        ),
        name="critic_step",
    )(*(pltpu.with_memory_space_constraint(a, pltpu.HBM) for a in (features[0], cotangent[0], w_spatial, w_first, w_second)))
    input_grad, grad_spatial, grad_first, grad_second = pl.pallas_call(
        finish,
        out_shape=(
            jax.ShapeDtypeStruct((ch, nf, nr, width), BF16),
            jax.ShapeDtypeStruct((3, 3, ch, ch), F32),
            jax.ShapeDtypeStruct((3, ch, ch), F32),
            jax.ShapeDtypeStruct((3, ch, ch), F32),
        ),
        in_specs=[here] * 3,
        out_specs=(far, far, far, far),
        scratch_shapes=[
            vmem((3, 3, ch, ch), F32), vmem((3, ch, ch), F32), vmem((3, ch, ch), F32), dma((4,)),
        ],
        compiler_params=pltpu.CompilerParams(vmem_limit_bytes=8 * 1024 * 1024),
        name="hand_out_results",
    )(packed1, packed2, block)
    return input_grad[None], grad_spatial, grad_first, grad_second


def solution(mesh):
    sizes = tuple(mesh.shape[axis] for axis in AXES)
    big = P("batch", None, "tm", "height", None)
    return jax.shard_map(
        functools.partial(per_device, sizes),
        mesh=mesh,
        in_specs=(big, big, P(), P(), P()),
        out_specs=(big, P(), P(), P()),
        check_vma=False,
    )
```

time: 62.4 us -> 47.4 us (0.76)
  local copies, waits for them, and re-layouts: 7.91 us -> 0 us
  Pallas kernels: 53.5 us -> 46.7 us
    pallas_call x1, Pallas kernels: 53.5 us -> 45.5 us  [per_device(): pl.pallas_call(functools.partial(kernel, sizes, scale), out_shape=(jax.Sh...]
    unnamed x14 -> x0, local copies, waits for them, and re-layouts: 7.91 us -> none
    pallas_call x0 -> x1, Pallas kernels: none -> 1.15 us  [per_device(): pl.pallas_call(finish, out_shape=(jax.ShapeDtypeStruct((ch, nf, nr, width...]
where the time goes in v2:
time: 47.4 us; the launch traced here: 47.3 us
  Pallas kernels  46.7 us (99%)
  between operations  0.64 us (1%)
    pallas_call x1, Pallas kernels, per_device(): pl.pallas_call(functools.partial(kernel, sizes, scale), out_shape=(jax.Sh...  45.5 us
    pallas_call x1, Pallas kernels, per_device(): pl.pallas_call(finish, out_shape=(jax.ShapeDtypeStruct((ch, nf, nr, width...  1.15 us

profile of v2, /device:TPU:1, one launch (start us, length us, event | category | flops | bytes accessed | tf_op | source)
XLA Modules:
  0.0 47.3 jit_solution(11237899438006113180)
XLA Ops:
  0.6 45.5 %critic_step.1 = (bf16[64,4,8,256]{3,2,1,0:T(8,128)(2,1)S(1)}, f32[192,128]{1,0:T(8,128)S(1)}, f32[288,128]{1,0:T(8,128)S(1)}) custom-call(bf16[64,4,8,256]{3,2,1,0:T(8,128)(2,1)} %bitcast.3, bf16[64,4,8,256]{3,2,1,0:T(8,128)(2,1)} %bitcast.4, bf16[3,3,64,64]{3,2,1,0:T(8,128)(2,1)} %ws_hbm.1, bf16[3,64,64]{2,1,0:T(8,128)(2,1)} %w1_hbm.1, ...), custom_call_target="tpu_custom_call" | custom-call | tf_op jit(solution)/shard_map/critic_step/pallas_call | solution.py:526
  46.2 1.2 %hand_out_results.1 = (bf16[64,4,8,256]{3,2,1,0:T(8,128)(2,1)}, f32[3,3,64,64]{3,2,1,0:T(8,128)}, f32[3,64,64]{2,1,0:T(8,128)}, f32[3,64,64]{2,1,0:T(8,128)}) custom-call(f32[192,128]{1,0:T(8,128)S(1)} %get-tuple-element.11.packed1, f32[288,128]{1,0:T(8,128)S(1)} %get-tuple-element.12.packed2, bf16[64,4,8,256]{3,2,1,0:T(8,128)(2,1)S(1)} %get-tuple-element.13.block), custom_call_target="tpu_custom_call" | custom-call | tf_op jit(solution)/shard_map/hand_out_results/pallas_call | solution.py:541

commit v3 on v2

--- a/solution.py
+++ b/solution.py
@@ -65,7 +65,7 @@
     WF, WB, W1F, W1B, W1F2, W1B2, W2B, PIN, POUT,
     pack1, pack2,
     a1s, a1r, b1r, c1r, a2s, a2r, b2r, c2r,
-    sem_in, sends, recvs, ars, arr,
+    sem_in, sends, recvs, ars, arr, known,
 ):
     ntm, nheight, nbatch = sizes
     nxy = nheight * nbatch
@@ -92,24 +92,53 @@
 
     barrier = pltpu.get_barrier_semaphore()
 
-    def greet_xy(d, _):
-        pl.semaphore_signal(barrier, inc=1, device_id=xy_device(lax.rem(me + d, nxy)), device_id_type=MESH)
-        return 0
-
-    def greet_tm(d, _):
-        pl.semaphore_signal(barrier, inc=1, device_id=tm_device(lax.rem(t + d, ntm)), device_id_type=MESH)
-        return 0
+    beside = (t, hh, nbatch - 1 - b)
+
+    def tell(sem, distance, along_tm):
+        if along_tm:
+            for d in (distance, ntm - distance):
+                pl.semaphore_signal(sem, inc=1, device_id=(lax.rem(t + d, ntm), hh, b), device_id_type=MESH)
+
+        @pl.when(hh >= distance)
+        def _():
+            pl.semaphore_signal(sem, inc=1, device_id=(t, hh - distance, b), device_id_type=MESH)
+
+        @pl.when(hh + distance < nheight)
+        def _():
+            pl.semaphore_signal(sem, inc=1, device_id=(t, hh + distance, b), device_id_type=MESH)
+
+    def hear(sem, distance, along_tm, others=0):
+        upper = (hh + nheight - distance) // nheight
+        lower = (2 * nheight - 1 - distance - hh) // nheight
+        pl.semaphore_wait(sem, upper + lower + 2 * along_tm + others)
+
+    rounds = [(n, d, d < ntm // 2) for n, d in enumerate((1, 2, 4)) if d < nheight or d < ntm // 2]
+
+    def pass_on(n):
+        if n > 0 and n <= len(rounds):
+            _, d, along_tm = rounds[n - 1]
+            hear(known.at[n - 1], d, along_tm)
+        if n < len(rounds):
+            _, d, along_tm = rounds[n]
+            tell(known.at[n], d, along_tm)
+        if n == 3 and nbatch == 2:
+            pl.semaphore_signal(known.at[3], inc=1, device_id=beside, device_id_type=MESH)
+        if n == 4 and nbatch == 2:
+            pl.semaphore_wait(known.at[3], 1)
 
     loads_w = [
         pltpu.make_async_copy(source, target, sem_in.at[2 * nf + n])
         for n, (source, target) in enumerate(((ws_hbm, ws), (w1_hbm, w1), (w2_hbm, w2)))
     ]
     loads_f = [pltpu.make_async_copy(feat.at[:, f], raw_f.at[f], sem_in.at[f]) for f in range(nf)]
-    loads_c = [pltpu.make_async_copy(cot.at[:, f], raw_c.at[f], sem_in.at[nf + f]) for f in range(nf)]
-    for copy in loads_w + loads_f + loads_c:
+    loads_c = [pltpu.make_async_copy(cot.at[:, f], raw_c.at[f + 2], sem_in.at[nf + f]) for f in range(nf)]
+    for copy in loads_w + loads_f:
         copy.start()
-    lax.fori_loop(1, nxy, greet_xy, 0)
-    lax.fori_loop(1, ntm, greet_tm, 0)
+    tell(barrier, 1, True)
+    if nbatch == 2:
+        pl.semaphore_signal(barrier, inc=1, device_id=beside, device_id_type=MESH)
+    for copy in loads_c:
+        copy.start()
 
     row = lax.broadcasted_iota(jnp.int32, (CH, 4 * CH), 0)
     col = lax.broadcasted_iota(jnp.int32, (CH, 4 * CH), 1)
@@ -173,22 +202,23 @@
         FI[s, f + 1] = act.astype(BF16)
         D1[at, h] = der
 
+    def cot_rows(k):
+        for part in range(2):
+            lanes = pl.ds(half * part, half)
+            block = to_rows(raw_c.at[k], part)
+            CT[0, k % 2, k // 2, lanes, :] = block[0]
+            CT[1, k % 2, k // 2, lanes, :] = block[nr - 1]
+            CT[pl.ds(2, nr - 2), k % 2, k // 2, lanes, :] = block[1 : nr - 1]
+
     for f in outer + inner:
         loads_f[f].wait()
         for part in range(2):
             X[place_of[f], pl.ds(1, nr), pl.ds(half * part, half), :] = to_rows(raw_f.at[f], part)
+    for f in outer:
         for h in range(1, nr - 1):
             conv_row(place_of[f], f, h, h + 1)
-    for f in range(nf):
-        loads_c[f].wait()
-        for part in range(2):
-            lanes = pl.ds(half * part, half)
-            block = to_rows(raw_c.at[f], part)
-            CT[0, f % 2, f // 2 + 1, lanes, :] = block[0]
-            CT[1, f % 2, f // 2 + 1, lanes, :] = block[nr - 1]
-            CT[pl.ds(2, nr - 2), f % 2, f // 2 + 1, lanes, :] = block[1 : nr - 1]
-
-    pl.semaphore_wait(barrier, nxy - 1 + ntm - 1)
+
+    hear(barrier, 1, True, nbatch - 1)
 
     used = [0]
 
@@ -210,15 +240,12 @@
             pl.when(has_below)(self.down.start)
 
         def wait(self):
-            @pl.when(has_above)
-            def _():
-                self.up.wait_send()
-                self.down.wait_recv()
-
-            @pl.when(has_below)
-            def _():
-                self.down.wait_send()
-                self.up.wait_recv()
+            pl.when(has_above)(self.down.wait_recv)
+            pl.when(has_below)(self.up.wait_recv)
+
+        def drain(self):
+            pl.when(has_above)(self.up.wait_send)
+            pl.when(has_below)(self.down.wait_send)
 
     class Frames:
         def __init__(self, back_src, back_dst, fore_src, fore_dst):
@@ -230,8 +257,11 @@
 
         def wait(self):
             for copy in self.both:
+                copy.wait_recv()
+
+        def drain(self):
+            for copy in self.both:
                 copy.wait_send()
-                copy.wait_recv()
 
     def outer_frames(array, rows):
         return Frames(array.at[rows, 1], array.at[rows, nf + 1], array.at[rows, nf], array.at[rows, 0])
@@ -240,15 +270,18 @@
     first_two, second_two = pl.ds(0, 2), pl.ds(2, 2)
     x_outer, x_inner = Rows(X, first_two), Rows(X, second_two)
     first_middle, first_edges = outer_frames(FI, middle), outer_frames(FI, edges)
-    cot_far = Frames(CT.at[:, 1, 1], CT.at[:, 1, 3], CT.at[:, 0, 2], CT.at[:, 0, 0])
-    cot_near = Frames(CT.at[:, 0, 1], CT.at[:, 0, 3], CT.at[:, 1, 2], CT.at[:, 1, 0])
+    cot_far = Frames(cot.at[:, 1], raw_c.at[nf + 3], cot.at[:, nf - 2], raw_c.at[0])
+    cot_near = Frames(cot.at[:, 0], raw_c.at[nf + 2], cot.at[:, nf - 1], raw_c.at[1])
     back_middle, back_edges = outer_frames(BS, middle), outer_frames(BS, edges)
     rows_inner, rows_outer = Rows(BF, second_two), Rows(BF, first_two)
 
     x_outer.start()
     first_middle.start()
     cot_far.start()
-    x_inner.start()
+    pass_on(0)
+    for f in inner:
+        for h in range(1, nr - 1):
+            conv_row(place_of[f], f, h, h + 1)
 
     def keep_second(f, s, value):
         act, der = gate(value)
@@ -271,7 +304,12 @@
 
     for s in range(2, nr):
         second_inner(s)
+    for f in range(nf):
+        loads_c[f].wait()
+        cot_rows(f + 2)
+    x_inner.start()
     cot_near.start()
+    pass_on(1)
     first_middle.wait()
     for s in range(2, nr):
         second_outer(s)
@@ -283,11 +321,14 @@
     first_edges.start()
 
     cot_far.wait()
+    cot_rows(0)
+    cot_rows(nf + 3)
     for s in range(2, nr):
         for f in outer:
             back_second(f, s)
     back_middle.start()
 
+    pass_on(2)
     x_inner.wait()
     for f in inner:
         conv_row(place_of[f], f, 0, 0)
@@ -302,7 +343,10 @@
             back_second(f, s)
     back_edges.start()
 
+    pass_on(3)
     cot_near.wait()
+    cot_rows(1)
+    cot_rows(nf + 2)
     for s in range(nr):
         for f in inner:
             back_second(f, s)
@@ -368,7 +412,6 @@
 
     def exchange_tm(send, recv, spread, which):
         await_all(recv, nxy - 1, arr.at[which])
-        await_all(send, nxy - 1, ars.at[which])
         spread[t] = added(recv)
 
         def one(d, _):
@@ -380,7 +423,6 @@
 
     def gather_xy(spread, gathered, which):
         await_all(spread, ntm - 1, arr.at[which + 1])
-        await_all(spread, ntm - 1, ars.at[which + 1])
         gathered[me] = added(spread)
 
         def one(d, _):
@@ -392,7 +434,6 @@
 
     def unpack(packed, gathered, which):
         await_all(gathered, nxy - 1, arr.at[which + 2])
-        await_all(gathered, nxy - 1, ars.at[which + 2])
         rows = gathered.shape[1]
         for g in range(nxy):
             packed[pl.ds(rows * g, rows), :] = gathered[g] * scale
@@ -418,6 +459,7 @@
     pack1[pl.ds(0, CH), :] = s1[:, : 2 * CH]
     pack1[pl.ds(CH, CH), :] = side_by_side(s1[:, 2 * CH :], s2[:CH])
     pack1[pl.ds(2 * CH, CH), :] = side_by_side(s2[CH : 2 * CH], s2[2 * CH :])
+    pass_on(4)
     reduce_scatter(pack1, a1s, a1r, 0)
 
     wide = [jnp.zeros((2 * CH, 4 * CH), F32)] * 3
@@ -454,7 +496,6 @@
     pack2[pl.ds(3 * CH, CH), :] = jnp.where(low, tails[0], tails[1])
     pack2[pl.ds(4 * CH, half), :] = jnp.where(low[:half], tails[2][:half], tails[2][half:])
     reduce_scatter(pack2, a2s, a2r, 3)
-    rows_outer.start()
     exchange_tm(a1s, a1r, b1r, 0)
 
     def grad_row(at, h):
@@ -477,6 +518,7 @@
 
     lax.fori_loop(0, nf, grad_inner, 0)
     exchange_tm(a2s, a2r, b2r, 3)
+    rows_outer.start()
     rows_inner.wait()
     for f in inner:
         hand_out(f)
@@ -487,6 +529,12 @@
     gather_xy(b2r, c2r, 3)
     unpack(out1, c1r, 0)
     unpack(out2, c2r, 3)
+    halos = (x_outer, x_inner, first_middle, first_edges, cot_far, cot_near)
+    for halo in halos + (back_middle, back_edges, rows_inner, rows_outer):
+        halo.drain()
+    for which, sent in ((0, (a1s, b1r, c1r)), (3, (a2s, b2r, c2r))):
+        for n, count in enumerate((nxy, ntm, nxy)):
+            await_all(sent[n], count - 1, ars.at[which + n])
 
 
 def per_device(sizes, features, cotangent, w_spatial, w_first, w_second):
@@ -501,7 +549,7 @@
     dma = pltpu.SemaphoreType.DMA
     scratch = [
         vmem((3, 3, ch, ch)), vmem((3, ch, ch)), vmem((3, ch, ch)),
-        vmem((nf, ch, nr, width)), vmem((nf, ch, nr, width)),
+        vmem((nf, ch, nr, width)), vmem((nf + 4, ch, nr, width)),
         vmem((nf, nr + 2, ch, width)),
         vmem((nr, nf + 2, ch, width)),
         vmem((nf, nr, ch, width), F32),
@@ -519,7 +567,7 @@
         vmem((ntm, rows1, 2 * ch), F32), vmem((nxy, rows1, 2 * ch), F32),
         vmem((nxy, rows2, 2 * ch), F32), vmem((nxy, rows2, 2 * ch), F32),
         vmem((ntm, rows2, 2 * ch), F32), vmem((nxy, rows2, 2 * ch), F32),
-        dma((2 * nf + 3,)), dma((20,)), dma((20,)), dma((6,)), dma((6,)),
+        dma((2 * nf + 3,)), dma((20,)), dma((20,)), dma((6,)), dma((6,)), pltpu.SemaphoreType.REGULAR((4,)),
     ]
     here = pl.BlockSpec(memory_space=pltpu.VMEM)
     far = pl.BlockSpec(memory_space=pltpu.HBM)

time: 47.4 us -> 45.1 us (0.951)
  Pallas kernels: 46.7 us -> 44.4 us
    pallas_call x1, Pallas kernels: 45.5 us -> 43.3 us  [per_device(): pl.pallas_call(functools.partial(kernel, sizes, scale), out_shape=(jax.Sh...]
where the time goes in v3:
time: 45.1 us; the launch traced here: 45 us
  Pallas kernels  44.4 us (98%)
  between operations  0.64 us (1%)
    pallas_call x1, Pallas kernels, per_device(): pl.pallas_call(functools.partial(kernel, sizes, scale), out_shape=(jax.Sh...  43.3 us
    pallas_call x1, Pallas kernels, per_device(): pl.pallas_call(finish, out_shape=(jax.ShapeDtypeStruct((ch, nf, nr, width...  1.15 us

profile of v3, /device:TPU:1, one launch (start us, length us, event | category | flops | bytes accessed | tf_op | source)
XLA Modules:
  0.0 45.0 jit_solution(14732074125145277481)
XLA Ops:
  0.6 43.3 %critic_step.1 = (bf16[64,4,8,256]{3,2,1,0:T(8,128)(2,1)S(1)}, f32[192,128]{1,0:T(8,128)S(1)}, f32[288,128]{1,0:T(8,128)S(1)}) custom-call(bf16[64,4,8,256]{3,2,1,0:T(8,128)(2,1)} %bitcast.3, bf16[64,4,8,256]{3,2,1,0:T(8,128)(2,1)} %bitcast.4, bf16[3,3,64,64]{3,2,1,0:T(8,128)(2,1)} %ws_hbm.1, bf16[3,64,64]{2,1,0:T(8,128)(2,1)} %w1_hbm.1, ...), custom_call_target="tpu_custom_call" | custom-call | tf_op jit(solution)/shard_map/critic_step/pallas_call | solution.py:574
  43.9 1.2 %hand_out_results.1 = (bf16[64,4,8,256]{3,2,1,0:T(8,128)(2,1)}, f32[3,3,64,64]{3,2,1,0:T(8,128)}, f32[3,64,64]{2,1,0:T(8,128)}, f32[3,64,64]{2,1,0:T(8,128)}) custom-call(f32[192,128]{1,0:T(8,128)S(1)} %get-tuple-element.11.packed1, f32[288,128]{1,0:T(8,128)S(1)} %get-tuple-element.12.packed2, bf16[64,4,8,256]{3,2,1,0:T(8,128)(2,1)S(1)} %get-tuple-element.13.block), custom_call_target="tpu_custom_call" | custom-call | tf_op jit(solution)/shard_map/hand_out_results/pallas_call | solution.py:589

commit v4 on v3

--- a/solution.py
+++ b/solution.py
@@ -282,6 +282,8 @@
     for f in inner:
         for h in range(1, nr - 1):
             conv_row(place_of[f], f, h, h + 1)
+    x_inner.start()
+    cot_near.start()
 
     def keep_second(f, s, value):
         act, der = gate(value)
@@ -307,8 +309,6 @@
     for f in range(nf):
         loads_c[f].wait()
         cot_rows(f + 2)
-    x_inner.start()
-    cot_near.start()
     pass_on(1)
     first_middle.wait()
     for s in range(2, nr):

time: 45.1 us -> 45.2 us (level)
  no operation moved by 1% of the time
where the time goes in v4:
time: 45.2 us; the launch traced here: 45.1 us
  Pallas kernels  44.4 us (98%)
  between operations  0.64 us (1%)
    pallas_call x1, Pallas kernels, per_device(): pl.pallas_call(functools.partial(kernel, sizes, scale), out_shape=(jax.Sh...  43.3 us
    pallas_call x1, Pallas kernels, per_device(): pl.pallas_call(finish, out_shape=(jax.ShapeDtypeStruct((ch, nf, nr, width...  1.15 us

profile of v4, /device:TPU:1, one launch (start us, length us, event | category | flops | bytes accessed | tf_op | source)
XLA Modules:
  0.0 45.1 jit_solution(15190796253021003592)
XLA Ops:
  0.6 43.3 %critic_step.1 = (bf16[64,4,8,256]{3,2,1,0:T(8,128)(2,1)S(1)}, f32[192,128]{1,0:T(8,128)S(1)}, f32[288,128]{1,0:T(8,128)S(1)}) custom-call(bf16[64,4,8,256]{3,2,1,0:T(8,128)(2,1)} %bitcast.3, bf16[64,4,8,256]{3,2,1,0:T(8,128)(2,1)} %bitcast.4, bf16[3,3,64,64]{3,2,1,0:T(8,128)(2,1)} %ws_hbm.1, bf16[3,64,64]{2,1,0:T(8,128)(2,1)} %w1_hbm.1, ...), custom_call_target="tpu_custom_call" | custom-call | tf_op jit(solution)/shard_map/critic_step/pallas_call | solution.py:574
  43.9 1.2 %hand_out_results.1 = (bf16[64,4,8,256]{3,2,1,0:T(8,128)(2,1)}, f32[3,3,64,64]{3,2,1,0:T(8,128)}, f32[3,64,64]{2,1,0:T(8,128)}, f32[3,64,64]{2,1,0:T(8,128)}) custom-call(f32[192,128]{1,0:T(8,128)S(1)} %get-tuple-element.11.packed1, f32[288,128]{1,0:T(8,128)S(1)} %get-tuple-element.12.packed2, bf16[64,4,8,256]{3,2,1,0:T(8,128)(2,1)S(1)} %get-tuple-element.13.block), custom_call_target="tpu_custom_call" | custom-call | tf_op jit(solution)/shard_map/hand_out_results/pallas_call | solution.py:589
